TPU v7x, 512 devices: a whole 4x4x16 slice. The times are simulated.
512 devices in a mesh: tile: 32 (over y, x, core), member: 16 (over z).
Axes of the slice: x: 4, y: 4, z: 16, core: 2. Of those that a mesh axis runs over, the one named last changes fastest.
Arguments:
- hx: bfloat16 [512, 131072], P('member', 'tile'), may hold values from -6 to 6
- obs_value: bfloat16 [131072], P('tile'), may hold values from -8 to 8
- obs_rinv: bfloat16 [131072], P('tile'), may hold values from 0.29882812 to 4
- obs_index: int32 [512, 1024], P('tile'), may hold values from 128 to 6015, as said below
- loc_weight: float32 [512, 1024], P(('tile', 'member')), may hold values from 0.05 to 1
- state: bfloat16 [512, 524288], P('member', 'tile'), may hold values from -6 to 6
Outputs:
- analysis: bfloat16 [512, 524288], P('member', 'tile')
Inputs may be any that keep to these rules, and one draw needn't show every extreme that they name: `obs_index`: row p lists 1024 distinct positions in the pool of tile p // 16: positions 0 .. 1023 are the last 1024 observations of the tile before it, the next 4096 the tile's own, the last 1024 the first observations of the tile after it; the tiles form a closed band. All positions of a row lie within 2048 consecutive positions.
All inputs are finite; a program needn't handle non-finite values.
Results may differ from a plain program's by a relative error of at most 0.012.
The roundings to bfloat16 on the way count: a program that leaves them out, or rounds other values in their place, can miss the bound.
Values may be sent and summed in bfloat16 or wider, within the bound.
A program may use at most 64 MiB of HBM per device.

v0:
```python
import jax
import jax.numpy as jnp
from jax import lax
from jax.sharding import PartitionSpec as P

LOC = 1024
NS_ITERS = 3


def with_halo(block, sides, width):
    for axis, dim in sides:
        count = lax.axis_size(axis)
        forward = [(i, i + 1) for i in range(count - 1)]
        forward.append((count - 1, 0))
        backward = [(target, source) for source, target in forward]
        low = lax.ppermute(
            lax.slice_in_dim(block, block.shape[dim] - width, None, axis=dim), axis, forward
        )
        high = lax.ppermute(lax.slice_in_dim(block, 0, width, axis=dim), axis, backward)
        block = jnp.concatenate([low, block, high], axis=dim)
    return block


def product_f32(left, right, dims):
    return lax.dot_general(
        left.astype(jnp.float32),
        right.astype(jnp.float32),
        (dims, ((), ())),
        precision=lax.Precision.HIGHEST,
        preferred_element_type=jnp.float32,
    )


def analysis(obs_block, obs_pair, loc_row):
    members = obs_block.shape[0]
    block_f = obs_block.astype(jnp.float32)
    obs_mean = jnp.mean(block_f, axis=0)
    obs_root = jnp.sqrt(obs_pair[1].astype(jnp.float32) * loc_row)
    scaled = ((block_f - obs_mean) * obs_root).astype(jnp.bfloat16)
    innovation = (obs_pair[0].astype(jnp.float32) - obs_mean) * obs_root
    gram_matrix = product_f32(scaled, scaled, ((1,), (1,)))
    identity = jnp.eye(members, dtype=jnp.float32)
    system = gram_matrix + (members - 1.0) * identity
    projection = jnp.dot(scaled.astype(jnp.float32), innovation, precision=lax.Precision.HIGHEST)
    norm_a = jnp.sqrt(jnp.sum(system * system))
    upper_iter = system / norm_a
    lower_iter = identity
    for sweep in range(NS_ITERS):
        upper_b = upper_iter.astype(jnp.bfloat16)
        lower_b = lower_iter.astype(jnp.bfloat16)
        product = product_f32(lower_b, upper_b, ((1,), (0,)))
        half_step = (1.5 * identity - 0.5 * product).astype(jnp.bfloat16)
        if sweep + 1 < NS_ITERS:
            upper_iter = product_f32(upper_b, half_step, ((1,), (0,)))
        lower_iter = product_f32(half_step, lower_b, ((1,), (0,)))
    invroot = lower_iter / jnp.sqrt(norm_a)
    inner_w = jnp.dot(invroot, projection, precision=lax.Precision.HIGHEST)
    mean_w = jnp.dot(invroot, inner_w, precision=lax.Precision.HIGHEST)
    transform = jnp.sqrt(members - 1.0) * invroot + mean_w[:, None]
    return transform.astype(jnp.bfloat16)


def transform_state(transform, state_block):
    block_f = state_block.astype(jnp.float32)
    state_mean = jnp.mean(block_f, axis=0)
    state_pert = (block_f - state_mean).astype(jnp.bfloat16)
    combined = product_f32(transform, state_pert, ((0,), (0,)))
    return (state_mean + combined).astype(jnp.bfloat16)


def on_device(hx, obs_value, obs_rinv, obs_index, loc_weight, state):
    ens_dev = hx.shape[0]
    member_pos = lax.axis_index("member")
    stacked = jnp.concatenate([hx, obs_value[None, :], obs_rinv[None, :]], axis=0)
    obs_pool = with_halo(stacked, (("tile", 1),), LOC)
    own_index = lax.dynamic_index_in_dim(obs_index, member_pos, 0, keepdims=False)
    obs_pair = jnp.take(obs_pool[ens_dev:], own_index, axis=1)
    all_rows = lax.all_gather(obs_pool[:ens_dev], "member", axis=0, tiled=True)
    obs_block = jnp.take(all_rows, own_index, axis=1)
    transform = analysis(obs_block, obs_pair, loc_weight[0])
    group_count = obs_index.shape[0]
    state_split = state.reshape(ens_dev, group_count, state.shape[1] // group_count)
    updated = transform_state(
        transform,
        lax.all_to_all(state_split, "member", split_axis=1, concat_axis=0, tiled=True)[:, 0, :],
    )
    result = lax.all_to_all(updated[:, None, :], "member", split_axis=0, concat_axis=1, tiled=True)
    return result.reshape(ens_dev, state.shape[1])


def solution(mesh):
    in_specs = (
        P("member", "tile"),
        P("tile"),
        P("tile"),
        P("tile", None),
        P(("tile", "member"), None),
        P("member", "tile"),
    )
    out_specs = P("member", "tile")
    return jax.shard_map(
        on_device, mesh=mesh, in_specs=in_specs, out_specs=out_specs, check_vma=False
    )
```

profile of v0, /device:TPU:16, one launch (start us, length us, event | category | flops | bytes accessed | tf_op | source)
XLA Modules:
  0.0 249.0 jit_solution(11522932096585671620)
XLA Ops:
  6.5 0.0 copy-start.1
  6.5 0.0 all-gather.2.cloned.1.call-start
  6.5 0.8 broadcast_in_dim.35
  7.3 0.7 broadcast_in_dim.36
  8.1 0.9 pad_maximum_fusion.3
  9.0 1.9 collective-permute-start
  10.9 5.8 %collective-permute-start.1 = (bf16[34,1024]{1,0:T(8,128)(2,1)S(1)}, bf16[34,1024]{1,0:T(8,128)(2,1)S(1)}, u32[]{:S(2)}, u32[]{:S(2)}) collective-permute-start(bf16[34,1024]{1,0:T(8,128)(2,1)S(1)} %get-tuple-element.8), channel_id=1, source_target_pairs={{16,0},{32,16},{48,32},{64,48},{80,64},{96,80},{112,96},{128,112},... | collective-permute-start | bytes 208904 | tf_op jit(solution)/shard_map/ppermute | solution.py:19
  16.6 0.2 collective-permute-done
  16.8 1.9 collective-permute-done.1
  18.7 1.0 pad_maximum_fusion
  19.7 0.8 slice.28
  20.5 0.0 all-gather.2.cloned.1.call-update
  20.5 0.0 copy-done.1
  20.5 0.0 copy-start
  20.5 1.1 copy.44
  21.6 15.2 %all-to-all-start = ((bf16[32,16,1024]{2,0,1:T(8,128)(2,1)}), bf16[32,16,1024]{2,0,1:T(8,128)(2,1)S(1)}, u32[]{:S(2)}, u32[]{:S(2)}) async-start(bf16[32,16,1024]{2,0,1:T(8,128)(2,1)} %bitcast.59), calls=%async_computation | async-start | bytes 2097152 | tf_op jit(solution)/shard_map/all_to_all | solution.py:85
  36.8 0.0 copy-start.2
  36.8 0.8 compare_select_fusion
  37.6 0.0 copy-done
  37.7 0.9 copy.34
  38.6 3.2 %gather_fusion.1 = bf16[1024,2]{1,0:T(8,128)(2,1)S(1)} fusion(bf16[2,6144]{0,1:T(8,128)(2,1)S(1)} %copy.34, s32[1024]{0:T(1024)S(1)} %broadcast_clamp_fusion), kind=kCustom, calls=%fused_computation.1 | custom fusion | bytes 12288 | tf_op jit(solution)/shard_map/jit(_take)/gather | solution.py:77
  41.8 0.2 select_bitcast_fusion
  42.0 0.1 slice.29
  42.1 0.1 copy.35
  42.3 0.0 copy-done.2
  42.3 0.2 copy.36
  42.5 0.1 convert_reduce_fusion.1
  42.7 0.2 sqrt_reduce_fusion
  42.9 53.0 %all-to-all-done = bf16[32,16,1024]{2,0,1:T(8,128)(2,1)S(1)} async-done(((bf16[32,16,1024]{2,0,1:T(8,128)(2,1)}), bf16[32,16,1024]{2,0,1:T(8,128)(2,1)S(1)}, u32[]{:S(2)}, u32[]{:S(2)}) %all-to-all-start) | async-done | bytes 1048608 | tf_op jit(solution)/shard_map/all_to_all | solution.py:85
  95.9 0.2 convert_reduce_fusion.2
  96.1 0.2 fusion.2
  96.4 54.4 %all-gather.2.cloned.1.call-done = bf16[512,6144]{1,0:T(8,128)(2,1)} async-done(((bf16[32,6144]{1,0:T(8,128)(2,1)}), bf16[512,6144]{1,0:T(8,128)(2,1)}) %all-gather.2.cloned.1.call-update) | async-done | bytes 6291472 | tf_op jit(solution)/shard_map/all_gather | solution.py:78
  150.8 8.6 %copy.33 = bf16[512,6144]{0,1:T(8,128)(2,1)} copy(bf16[512,6144]{1,0:T(8,128)(2,1)} %all-gather.2.cloned.1.call-done) | data formatting | bytes 12582912 | tf_op jit(solution)/shard_map/all_gather | solution.py:78
  159.4 7.6 %gather_fusion = bf16[1024,512]{1,0:T(8,128)(2,1)S(1)} fusion(bf16[512,6144]{0,1:T(8,128)(2,1)} %copy.33, s32[1024]{0:T(1024)S(1)} %broadcast_clamp_fusion), kind=kCustom, calls=%fused_computation | custom fusion | bytes 2101248 | tf_op jit(solution)/shard_map/jit(_take)/gather | solution.py:79
  167.0 0.5 convert_reduce_fusion
  167.5 0.9 fusion.1
  168.4 1.5 multiply_reduce_fusion
  170.7 0.4 fusion.4
  171.1 0.4 convolution_convert_fusion.2
  171.5 0.4 convolution_convert_fusion.3
  172.0 0.4 fusion.5
  172.4 0.4 convolution_convert_fusion.1
  172.9 0.4 convolution_convert_fusion
  173.3 0.5 convolution_bitcast_fusion.1
  173.8 0.5 fusion.6
  174.3 0.4 convolution_divide_fusion
  174.7 1.0 convolution_bitcast_fusion
  175.7 1.0 fusion.11
  176.7 0.8 fusion.3
  177.5 0.5 broadcast.96
  178.1 1.4 reduce.8
  179.5 0.8 reshape.88
  180.3 59.4 %all_to_all.24 = bf16[16,2,16384]{2,1,0:T(2,128)(2,1)S(1)} all-to-all(bf16[16,2,16384]{2,1,0:T(2,128)(2,1)S(1)} %reshape.88), channel_id=1, replica_groups=mesh['tile'=32,'member'=16] {'member'}, dimensions={0} | all-to-all | bytes 2097152 | tf_op jit(solution)/shard_map/all_to_all | solution.py:87
  239.7 1.0 reshape.89
  240.7 0.4 copy.39
  241.1 1.1 copy.41
  (6 shorter events, 0.1 us)
Async XLA Ops:
  6.5 14.0 %copy-start.1 = (bf16[32,16384]{1,0:T(8,128)(2,1)S(1)}, bf16[32,16384]{1,0:T(8,128)(2,1)}, u32[]{:S(2)}) copy-start(bf16[32,16384]{1,0:T(8,128)(2,1)} %param.11) | copy-start | bytes 3145732
  6.5 144.3 %all-gather.2.cloned.1.call-start = ((), (), s32[]{:S(2)}) async-start(), calls=%async_computation.2 | async-start | bytes 6684672 | tf_op jit(solution)/shard_map/all_gather | solution.py:78
  9.0 7.9 %collective-permute-start = (bf16[34,1024]{1,0:T(8,128)(2,1)S(1)}, bf16[34,1024]{1,0:T(8,128)(2,1)S(1)}, u32[]{:S(2)}, u32[]{:S(2)}) collective-permute-start(bf16[34,1024]{1,0:T(8,128)(2,1)S(1)} %get-tuple-element.7), channel_id=1, source_target_pairs={{0,16},{16,32},{32,48},{48,64},{64,80},{80,96},{96,112},{112,128},... | collective-permute-start | bytes 208904 | tf_op jit(solution)/shard_map/ppermute | solution.py:16
  10.9 7.8 %collective-permute-start.1 = (bf16[34,1024]{1,0:T(8,128)(2,1)S(1)}, bf16[34,1024]{1,0:T(8,128)(2,1)S(1)}, u32[]{:S(2)}, u32[]{:S(2)}) collective-permute-start(bf16[34,1024]{1,0:T(8,128)(2,1)S(1)} %get-tuple-element.8), channel_id=1, source_target_pairs={{16,0},{32,16},{48,32},{64,48},{80,64},{96,80},{112,96},{128,112},... | collective-permute-start | bytes 208904 | tf_op jit(solution)/shard_map/ppermute | solution.py:19
  20.5 17.1 %copy-start = (bf16[32,4096]{1,0:T(8,128)(2,1)S(1)}, bf16[32,4096]{1,0:T(8,128)(2,1)}, u32[]{:S(2)}) copy-start(bf16[32,4096]{1,0:T(8,128)(2,1)} %param.6) | copy-start | bytes 786436
  21.6 74.3 %all-to-all-start = ((bf16[32,16,1024]{2,0,1:T(8,128)(2,1)}), bf16[32,16,1024]{2,0,1:T(8,128)(2,1)S(1)}, u32[]{:S(2)}, u32[]{:S(2)}) async-start(bf16[32,16,1024]{2,0,1:T(8,128)(2,1)} %bitcast.59), calls=%async_computation | async-start | bytes 2097152 | tf_op jit(solution)/shard_map/all_to_all | solution.py:85
  36.8 5.5 %copy-start.2 = (f32[1,1024]{1,0:T(1,128)S(1)}, f32[1,1024]{1,0:T(1,128)}, u32[]{:S(2)}) copy-start(f32[1,1024]{1,0:T(1,128)} %param.10) | copy-start | bytes 12292
Sparse Core Ops, SparseCore 0:
  20.6 130.1 all-gather.1
where the time goes:
time: 250 us; the launch traced here: 249 us
  waiting for transfers between devices  110 us (44%)
  blocking collectives  59.4 us (24%)
  local copies, waits for them, and re-layouts  28.2 us (11%)
  starting transfers between devices  22.9 us (9%)
  between operations  14.4 us (6%)
  matrix products  8.3 us (3%)
  other arithmetic  6.37 us (3%)
    all_to_all x1, blocking collectives, on_device(): lax.all_to_all(updated[:, None, :], 'member', split_axis=0, concat_axis=1...  59.4 us
    all_gather x1, waiting for transfers between devices, on_device(): all_rows = lax.all_gather(obs_pool[:ens_dev], 'member', axis=0, tiled=True)  54.4 us
    all_to_all x1, waiting for transfers between devices, on_device(): lax.all_to_all(state_split, 'member', split_axis=1, concat_axis=0, tiled=...  53 us
    all_to_all x1, starting transfers between devices, on_device(): lax.all_to_all(state_split, 'member', split_axis=1, concat_axis=0, tiled=...  15.2 us
    all_gather x1, local copies, waits for them, and re-layouts, on_device(): all_rows = lax.all_gather(obs_pool[:ens_dev], 'member', axis=0, tiled=True)  8.64 us
    gather x1, local copies, waits for them, and re-layouts, on_device(): obs_block = jnp.take(all_rows, own_index, axis=1)  7.58 us
    dot_general x10, matrix products, product_f32(): lax.dot_general(left.astype(jnp.float32), right.astype(jnp.float32), (dim...  5.82 us
    ppermute x1, starting transfers between devices, with_halo(): lax.ppermute(lax.slice_in_dim(block, 0, width, axis=dim), axis, backward)  5.75 us
  transfers between devices with their start and end apart: 4, of which 4 were waited for; matrix products, arithmetic and copies ran while one was open for 3% of the time, Pallas kernels for 0%

commit v1 on v0

--- a/solution.py
+++ b/solution.py
@@ -75,7 +75,11 @@
     obs_pool = with_halo(stacked, (("tile", 1),), LOC)
     own_index = lax.dynamic_index_in_dim(obs_index, member_pos, 0, keepdims=False)
     obs_pair = jnp.take(obs_pool[ens_dev:], own_index, axis=1)
-    all_rows = lax.all_gather(obs_pool[:ens_dev], "member", axis=0, tiled=True)
+    x = obs_pool[:ens_dev]
+    count_2 = lax.axis_size("member")
+    pieces = jnp.stack([x for _ in range(count_2)])
+    pieces = lax.all_to_all(pieces, "member", split_axis=0, concat_axis=0)
+    all_rows = jnp.concatenate(pieces, axis=0)
     obs_block = jnp.take(all_rows, own_index, axis=1)
     transform = analysis(obs_block, obs_pair, loc_weight[0])
     group_count = obs_index.shape[0]

time: 250 us -> 450 us (1.80)
  waiting for transfers between devices: 110 us -> 308 us
  between operations: 14.4 us -> 1.1 us
  starting transfers between devices: 22.9 us -> 30.8 us
    all_to_all x0 -> x1, waiting for transfers between devices: none -> 266 us  [on_device(): pieces = lax.all_to_all(pieces, 'member', split_axis=0, concat_axis=0)]
    all_gather x1 -> x0, waiting for transfers between devices: 54.4 us -> none  [on_device(): all_rows = lax.all_gather(obs_pool[:ens_dev], 'member', axis=0, tiled=True)]
    all_to_all x1, waiting for transfers between devices: 53 us -> 40.1 us  [on_device(): lax.all_to_all(state_split, 'member', split_axis=1, concat_axis=0, tiled=...]
    reshape x0 -> x1, local copies, waits for them, and re-layouts: none -> 8.64 us  [on_device(): all_rows = jnp.concatenate(pieces, axis=0)]
    all_gather x1 -> x0, local copies, waits for them, and re-layouts: 8.64 us -> none  [on_device(): all_rows = lax.all_gather(obs_pool[:ens_dev], 'member', axis=0, tiled=True)]
    all_to_all x0 -> x1, starting transfers between devices: none -> 7.92 us  [on_device(): pieces = lax.all_to_all(pieces, 'member', split_axis=0, concat_axis=0)]
  transfers between devices with their start and end apart: 4 -> 4, of which waited for: 4 -> 4; matrix products, arithmetic and copies ran while one was open for 3% -> 1% of each run, Pallas kernels for 0% -> 0%
where the time goes in v1:
time: 450 us; the launch traced here: 449 us
  waiting for transfers between devices  308 us (68%)
  blocking collectives  62.2 us (14%)
  starting transfers between devices  30.8 us (7%)
  local copies, waits for them, and re-layouts  30.4 us (7%)
  matrix products  11.7 us (3%)
  other arithmetic  4.71 us (1%)
    all_to_all x1, waiting for transfers between devices, on_device(): pieces = lax.all_to_all(pieces, 'member', split_axis=0, concat_axis=0)  266 us
    all_to_all x1, blocking collectives, on_device(): lax.all_to_all(updated[:, None, :], 'member', split_axis=0, concat_axis=1...  62.2 us
    all_to_all x1, waiting for transfers between devices, on_device(): lax.all_to_all(state_split, 'member', split_axis=1, concat_axis=0, tiled=...  40.1 us
    all_to_all x1, starting transfers between devices, on_device(): lax.all_to_all(state_split, 'member', split_axis=1, concat_axis=0, tiled=...  15.2 us
    dot_general x10, matrix products, product_f32(): lax.dot_general(left.astype(jnp.float32), right.astype(jnp.float32), (dim...  9.17 us
  transfers between devices with their start and end apart: 4, of which 4 were waited for; matrix products, arithmetic and copies ran while one was open for 1% of the time, Pallas kernels for 0%

profile of v1, /device:TPU:16, one launch (start us, length us, event | category | flops | bytes accessed | tf_op | source)
XLA Modules:
  0.0 448.8 jit_solution(3487662305579844857)
XLA Ops:
  0.0 0.0 copy-start.1
  0.0 0.0 copy-start.2
  0.0 0.0 copy-start
  0.0 2.3 copy.46
  2.3 15.2 %all-to-all-start = ((bf16[32,16,1024]{2,0,1:T(8,128)(2,1)}), bf16[32,16,1024]{2,0,1:T(8,128)(2,1)S(1)}, u32[]{:S(2)}, u32[]{:S(2)}) async-start(bf16[32,16,1024]{2,0,1:T(8,128)(2,1)} %bitcast.60), calls=%async_computation | async-start | bytes 2097152 | tf_op jit(solution)/shard_map/all_to_all | solution.py:89
  17.5 0.0 copy-done.1
  17.6 0.0 copy-done.2
  17.6 0.0 copy-done
  17.6 1.9 collective-permute-start
  19.6 5.8 %collective-permute-start.1 = (bf16[34,1024]{1,0:T(8,128)(2,1)S(1)}, bf16[34,1024]{1,0:T(8,128)(2,1)S(1)}, u32[]{:S(2)}, u32[]{:S(2)}) collective-permute-start(bf16[34,1024]{1,0:T(8,128)(2,1)S(1)} %get-tuple-element.8), channel_id=1, source_target_pairs={{16,0},{32,16},{48,32},{64,48},{80,64},{96,80},{112,96},{128,112},... | collective-permute-start | bytes 208904 | tf_op jit(solution)/shard_map/ppermute | solution.py:19
  25.3 0.2 collective-permute-done
  25.5 1.9 collective-permute-done.1
  27.4 0.1 pad_maximum_fusion
  27.5 40.1 %all-to-all-done = bf16[32,16,1024]{2,0,1:T(8,128)(2,1)S(1)} async-done(((bf16[32,16,1024]{2,0,1:T(8,128)(2,1)}), bf16[32,16,1024]{2,0,1:T(8,128)(2,1)S(1)}, u32[]{:S(2)}, u32[]{:S(2)}) %all-to-all-start) | async-done | bytes 1048608 | tf_op jit(solution)/shard_map/all_to_all | solution.py:89
  67.5 3.4 stack.2
  70.9 7.9 %all-to-all-start.1 = ((bf16[16,32,6144]{2,1,0:T(8,128)(2,1)}), bf16[16,32,6144]{2,1,0:T(8,128)(2,1)}, u32[]{:S(2)}, u32[]{:S(2)}) async-start(bf16[16,32,6144]{2,1,0:T(8,128)(2,1)} %stack.2), calls=%async_computation.1 | async-start | bytes 12582912 | tf_op jit(solution)/shard_map/all_to_all | solution.py:81
  78.9 0.0 copy-start.3
  78.9 0.8 compare_select_fusion
  79.7 0.9 copy.36
  80.6 3.2 gather_fusion.1
  83.8 0.2 select_bitcast_fusion
  84.1 0.1 slice.29
  84.2 0.1 copy.37
  84.3 0.0 copy-done.3
  84.4 0.2 copy.38
  84.6 0.3 convert_reduce_fusion.1
  84.9 0.2 convert_reduce_fusion.2
  85.1 0.2 fusion.2
  85.3 265.9 %all-to-all-done.1 = bf16[16,32,6144]{2,1,0:T(8,128)(2,1)} async-done(((bf16[16,32,6144]{2,1,0:T(8,128)(2,1)}), bf16[16,32,6144]{2,1,0:T(8,128)(2,1)}, u32[]{:S(2)}, u32[]{:S(2)}) %all-to-all-start.1) | async-done | bytes 6291488 | tf_op jit(solution)/shard_map/all_to_all | solution.py:81
  351.2 8.6 %copy.35 = bf16[512,6144]{0,1:T(8,128)(2,1)} copy(bf16[512,6144]{1,0:T(8,128)(2,1)} %bitcast.1) | data formatting | bytes 12582912 | tf_op jit(solution)/shard_map/reshape | solution.py:82
  359.9 7.6 %gather_fusion = bf16[1024,512]{1,0:T(8,128)(2,1)S(1)} fusion(bf16[512,6144]{0,1:T(8,128)(2,1)} %copy.35, s32[1024]{0:T(1024)S(1)} %broadcast_clamp_fusion), kind=kCustom, calls=%fused_computation | custom fusion | bytes 2101248 | tf_op jit(solution)/shard_map/jit(_take)/gather | solution.py:83
  367.5 0.5 convert_reduce_fusion
  368.0 0.9 fusion.1
  368.9 2.4 multiply_reduce_fusion
  372.0 1.7 fusion.4
  373.7 1.7 convolution_convert_fusion.2
  375.3 0.4 convolution_convert_fusion.3
  375.8 0.4 fusion.5
  376.2 0.4 convolution_convert_fusion
  376.6 0.4 convolution_convert_fusion.1
  377.1 0.5 convolution_bitcast_fusion.1
  377.6 0.5 fusion.6
  378.1 0.4 convolution_divide_fusion
  378.5 1.0 convolution_bitcast_fusion
  379.5 1.0 fusion.11
  380.5 0.8 fusion.3
  381.4 0.5 broadcast.98
  381.9 1.4 reduce.8
  383.3 0.8 reshape.94
  384.1 62.2 %all_to_all.29 = bf16[16,2,16384]{2,1,0:T(2,128)(2,1)S(1)} all-to-all(bf16[16,2,16384]{2,1,0:T(2,128)(2,1)S(1)} %reshape.94), channel_id=1, replica_groups=mesh['tile'=32,'member'=16] {'member'}, dimensions={0} | all-to-all | bytes 2097152 | tf_op jit(solution)/shard_map/all_to_all | solution.py:91
  446.3 1.0 reshape.95
  447.4 0.4 copy.41
  447.8 1.1 copy.43
  (10 shorter events, 0.2 us)
Async XLA Ops:
  0.0 17.5 %copy-start.1 = (bf16[4096]{0:T(1024)(128)(2,1)S(1)}, bf16[4096]{0:T(1024)(128)(2,1)}, u32[]{:S(2)}) copy-start(bf16[4096]{0:T(1024)(128)(2,1)} %param.7) | copy-start | bytes 24580
  0.0 17.6 %copy-start.2 = (bf16[4096]{0:T(1024)(128)(2,1)S(1)}, bf16[4096]{0:T(1024)(128)(2,1)}, u32[]{:S(2)}) copy-start(bf16[4096]{0:T(1024)(128)(2,1)} %param.8) | copy-start | bytes 24580
  0.0 17.6 %copy-start = (bf16[32,4096]{1,0:T(8,128)(2,1)S(1)}, bf16[32,4096]{1,0:T(8,128)(2,1)}, u32[]{:S(2)}) copy-start(bf16[32,4096]{1,0:T(8,128)(2,1)} %param.6) | copy-start | bytes 786436
  2.3 65.2 %all-to-all-start = ((bf16[32,16,1024]{2,0,1:T(8,128)(2,1)}), bf16[32,16,1024]{2,0,1:T(8,128)(2,1)S(1)}, u32[]{:S(2)}, u32[]{:S(2)}) async-start(bf16[32,16,1024]{2,0,1:T(8,128)(2,1)} %bitcast.60), calls=%async_computation | async-start | bytes 2097152 | tf_op jit(solution)/shard_map/all_to_all | solution.py:89
  17.6 7.9 %collective-permute-start = (bf16[34,1024]{1,0:T(8,128)(2,1)S(1)}, bf16[34,1024]{1,0:T(8,128)(2,1)S(1)}, u32[]{:S(2)}, u32[]{:S(2)}) collective-permute-start(bf16[34,1024]{1,0:T(8,128)(2,1)S(1)} %get-tuple-element.7), channel_id=1, source_target_pairs={{0,16},{16,32},{32,48},{48,64},{64,80},{80,96},{96,112},{112,128},... | collective-permute-start | bytes 208904 | tf_op jit(solution)/shard_map/ppermute | solution.py:16
  19.6 7.8 %collective-permute-start.1 = (bf16[34,1024]{1,0:T(8,128)(2,1)S(1)}, bf16[34,1024]{1,0:T(8,128)(2,1)S(1)}, u32[]{:S(2)}, u32[]{:S(2)}) collective-permute-start(bf16[34,1024]{1,0:T(8,128)(2,1)S(1)} %get-tuple-element.8), channel_id=1, source_target_pairs={{16,0},{32,16},{48,32},{64,48},{80,64},{96,80},{112,96},{128,112},... | collective-permute-start | bytes 208904 | tf_op jit(solution)/shard_map/ppermute | solution.py:19
  70.9 280.3 %all-to-all-start.1 = ((bf16[16,32,6144]{2,1,0:T(8,128)(2,1)}), bf16[16,32,6144]{2,1,0:T(8,128)(2,1)}, u32[]{:S(2)}, u32[]{:S(2)}) async-start(bf16[16,32,6144]{2,1,0:T(8,128)(2,1)} %stack.2), calls=%async_computation.1 | async-start | bytes 12582912 | tf_op jit(solution)/shard_map/all_to_all | solution.py:81
  78.9 5.5 %copy-start.3 = (f32[1,1024]{1,0:T(1,128)S(1)}, f32[1,1024]{1,0:T(1,128)}, u32[]{:S(2)}) copy-start(f32[1,1024]{1,0:T(1,128)} %param.10) | copy-start | bytes 12292
